TPU v7x, 256 devices: a whole 4x4x8 slice. The times are simulated.
256 devices in a mesh: tok: 32 (over x_lo, z, core), feat: 8 (over x_hi, y).
Axes of the slice: x: 4 (x_hi: 2, x_lo: 2; x = x_hi * 2 + x_lo), y: 4, z: 8, core: 2. Of those that a mesh axis runs over, the one named last changes fastest.
Arguments:
- teacher: bfloat16 [8192, 8192], P('tok', 'feat')
- student: bfloat16 [8192, 5120], P('tok', 'feat')
Outputs:
- loss: float32 [], replicated
- grad_student: float32 [8192, 5120], P('tok', 'feat')
All inputs are finite; a program needn't handle non-finite values.
Results may differ from a plain program's by a relative error of at most 0.0031.
Values may be sent and summed in bfloat16 or wider, within the bound.
A program may use at most 128 MiB of HBM per device.

v0:
```python
import jax
import jax.numpy as jnp
from jax import lax
from jax.sharding import PartitionSpec as P

DS = 5120


def gram_tile(rows, mine):
    return lax.dot_general(rows, mine, (((1,), (1,)), ((), ())), preferred_element_type=jnp.float32)


def local(teacher, student):
    width = teacher.shape[0]
    all_teacher, all_student = (
        lax.all_gather(teacher, "tok", axis=0, tiled=True),
        lax.all_gather(student, "tok", axis=0, tiled=True),
    )
    parts = lax.psum_scatter(
        jnp.concatenate([gram_tile(all_teacher, teacher), gram_tile(all_student, student)], axis=1),
        "feat",
        scatter_dimension=0,
        tiled=True,
    )
    kern = parts[:, :width]
    lern = parts[:, width:]
    local_sums = (jnp.sum(kern * lern), jnp.sum(kern * kern), jnp.sum(lern * lern))
    cross, ksq, lsq = lax.psum((local_sums[0], local_sums[1], local_sums[2]), ("tok", "feat"))
    knorm = jnp.sqrt(ksq)
    lnorm = jnp.sqrt(lsq)
    loss = -cross / (knorm * lnorm)
    weights = (-kern / (knorm * lnorm) + cross * lern / (knorm * lnorm**3)).astype(jnp.bfloat16)
    full_weights = lax.all_gather(weights, "feat", axis=0, tiled=True)
    scale = 2.0 * all_student.shape[0] * DS
    grad_student = scale * lax.dot_general(
        full_weights, all_student, (((0,), (0,)), ((), ())), preferred_element_type=jnp.float32
    )
    return (loss, grad_student)


def solution(mesh):
    placed = (P("tok", "feat"), P("tok", "feat"))
    return jax.shard_map(
        local, mesh=mesh, in_specs=placed, out_specs=(P(), P("tok", "feat")), check_vma=False
    )
```

profile of v0, /device:TPU:1, one launch (start us, length us, event | category | flops | bytes accessed | tf_op | source)
XLA Modules:
  0.0 575.2 jit_solution(16910604198474393018)
XLA Ops:
  7.2 0.0 all-gather.6.cloned.1.call-start
  7.2 0.7 all-gather.6.cloned.1.call-update
  7.9 0.0 all-gather.4.cloned.1.call-start
  7.9 0.7 all-gather.4.cloned.1.call-update
  8.6 0.0 copy-start.1
  8.7 0.0 reduce-scatter.2.cloned.1.call-start
  8.7 80.1 %all-gather.6.cloned.1.call-done = bf16[8192,640]{1,0:T(8,128)(2,1)} async-done(((bf16[256,640]{1,0:T(8,128)(2,1)}), bf16[8192,640]{1,0:T(8,128)(2,1)}) %all-gather.6.cloned.1.call-update) | async-done | bytes 10485776 | tf_op jit(solution)/shard_map/all_gather | solution.py:17
  88.8 10.7 %fusion.1 = f32[8192,256]{0,1:T(8,128)} fusion(bf16[8192,640]{1,0:T(8,128)(2,1)} %all-gather.6.cloned.1.call-done, bf16[256,640]{1,0:T(8,128)(2,1)} %param.3), kind=kOutput, calls=%fused_computation.7 | convolution fusion | flops 2684354560 | bytes 19202048 | tf_op jit(solution)/shard_map/dot_general | solution.py:10
  99.5 90.2 %all-gather.4.cloned.1.call-done = bf16[8192,1024]{1,0:T(8,128)(2,1)} async-done(((bf16[256,1024]{1,0:T(8,128)(2,1)}), bf16[8192,1024]{1,0:T(8,128)(2,1)}) %all-gather.4.cloned.1.call-update) | async-done | bytes 16777232 | tf_op jit(solution)/shard_map/all_gather | solution.py:16
  189.8 0.0 copy-done.1
  189.8 0.0 copy-start
  189.8 8.3 %fusion = f32[8192,256]{0,1:T(8,128)S(1)} fusion(bf16[8192,1024]{1,0:T(8,128)(2,1)} %all-gather.4.cloned.1.call-done, bf16[256,1024]{1,0:T(8,128)(2,1)S(1)} %copy-done.1), kind=kOutput, calls=%fused_computation.6 | convolution fusion | flops 4294967296 | bytes 25690112 | tf_op jit(solution)/shard_map/dot_general | solution.py:10
  198.1 0.0 copy-done
  198.1 6.2 %pad_maximum_fusion = f32[8192,512]{0,1:T(8,128)} fusion(f32[8192,256]{0,1:T(8,128)S(1)} %copy-done, f32[8192,256]{0,1:T(8,128)S(1)} %fusion), kind=kLoop, calls=%fused_computation | loop fusion | flops 4194304 | bytes 33554432 | tf_op jit(solution)/shard_map/concatenate | solution.py:20
  204.3 0.0 reduce-scatter.2.cloned.1.call-update
  204.3 0.0 all-gather.8.cloned.1.call-start
  204.4 195.3 %reduce-scatter.2.cloned.1.call-done = f32[1024,512]{0,1:T(8,128)} async-done(((f32[8192,512]{0,1:T(8,128)}), f32[1024,512]{0,1:T(8,128)}) %reduce-scatter.2.cloned.1.call-update) | async-done | bytes 2097168 | tf_op jit(solution)/shard_map/reduce_scatter | solution.py:19
  399.7 2.4 multiply_reduce_fusion
  402.1 78.7 %all-reduce = (f32[]{:T(128)}, f32[]{:T(128)}, f32[]{:T(128)}) all-reduce(f32[]{:T(128)} %get-tuple-element.3, f32[]{:T(128)} %get-tuple-element.4, f32[]{:T(128)} %get-tuple-element.2), channel_id=1, replica_groups=mesh['tok'=32,'feat'=8] {'tok','feat'}, use_global_device_ids=true, to_apply=%region_2.0 | all-reduce | flops 3 | bytes 24 | tf_op jit(solution)/shard_map/psum | solution.py:28
  482.2 3.3 add_convert_fusion
  485.5 0.0 all-gather.8.cloned.1.call-update
  486.3 71.7 %all-gather.8.cloned.1.call-done = bf16[8192,256]{0,1:T(8,128)(2,1)} async-done(((bf16[1024,256]{0,1:T(8,128)(2,1)}), bf16[8192,256]{0,1:T(8,128)(2,1)}) %all-gather.8.cloned.1.call-update) | async-done | bytes 4194320 | tf_op jit(solution)/shard_map/all_gather | solution.py:33
  558.0 9.5 %convolution_multiply_fusion = f32[256,640]{1,0:T(8,128)} fusion(bf16[8192,256]{0,1:T(8,128)(2,1)} %all-gather.8.cloned.1.call-done, bf16[8192,640]{1,0:T(8,128)(2,1)} %all-gather.6.cloned.1.call-done), kind=kOutput, calls=%fused_computation.1 | convolution fusion | flops 2684518400 | bytes 15335424 | tf_op jit(solution)/shard_map/dot_general | solution.py:35
Async XLA Ops:
  7.2 81.7 %all-gather.6.cloned.1.call-start = ((), (), s32[]{:S(2)}) async-start(), calls=%async_computation.2 | async-start | bytes 10813440 | tf_op jit(solution)/shard_map/all_gather | solution.py:17
  7.9 181.9 %all-gather.4.cloned.1.call-start = ((), (), s32[]{:S(2)}) async-start(), calls=%async_computation.1 | async-start | bytes 17301504 | tf_op jit(solution)/shard_map/all_gather | solution.py:16
  8.6 181.1 %copy-start.1 = (bf16[256,1024]{1,0:T(8,128)(2,1)S(1)}, bf16[256,1024]{1,0:T(8,128)(2,1)}, u32[]{:S(2)}) copy-start(bf16[256,1024]{1,0:T(8,128)(2,1)} %param.2) | copy-start | bytes 1572868
  8.7 391.0 %reduce-scatter.2.cloned.1.call-start = ((), (), s32[]{:S(2)}) async-start(), calls=%async_computation.3 | async-start | bytes 18874368 | tf_op jit(solution)/shard_map/reduce_scatter | solution.py:19
  189.8 8.3 %copy-start = (f32[8192,256]{0,1:T(8,128)S(1)}, f32[8192,256]{0,1:T(8,128)}, u32[]{:S(2)}) copy-start(f32[8192,256]{0,1:T(8,128)} %fusion.1) | copy-start | bytes 25165828
  204.3 353.6 %all-gather.8.cloned.1.call-start = ((), (), s32[]{:S(2)}) async-start(), calls=%async_computation.4 | async-start | bytes 4718592 | tf_op jit(solution)/shard_map/all_gather | solution.py:33
Sparse Core Ops, SparseCore 0:
  9.9 78.9 all-gather.5
  90.7 99.0 all-gather.3
  204.5 195.1 reduce-scatter.1
  485.6 72.2 all-gather.7
where the time goes:
time: 575 us
  waiting for transfers between devices  439 us (76%)
  blocking collectives  78.7 us (14%)
  matrix products  28.5 us (5%)
  between operations  17 us (3%)
  other arithmetic  11.9 us (2%)
    reduce_scatter x1, waiting for transfers between devices, local(): lax.psum_scatter(jnp.concatenate([gram_tile(all_teacher, teacher), gram_t...  195 us
    all_gather x1, waiting for transfers between devices, local(): lax.all_gather(teacher, 'tok', axis=0, tiled=True)  90.2 us
    all_gather x1, waiting for transfers between devices, local(): lax.all_gather(student, 'tok', axis=0, tiled=True)  80.1 us
    psum x1, blocking collectives, local(): lax.psum((local_sums[0], local_sums[1], local_sums[2]), ('tok', 'feat'))  78.7 us
    all_gather x1, waiting for transfers between devices, local(): full_weights = lax.all_gather(weights, 'feat', axis=0, tiled=True)  71.7 us
    dot_general x2, matrix products, gram_tile(): lax.dot_general(rows, mine, (((1,), (1,)), ((), ())), preferred_element_t...  19 us
  transfers between devices with their start and end apart: 4, of which 4 were waited for; matrix products, arithmetic and copies ran while one was open for 2% of the time, Pallas kernels for 0%

commit v1 on v0

--- a/solution.py
+++ b/solution.py
@@ -30,7 +30,9 @@
     lnorm = jnp.sqrt(lsq)
     loss = -cross / (knorm * lnorm)
     weights = (-kern / (knorm * lnorm) + cross * lern / (knorm * lnorm**3)).astype(jnp.bfloat16)
-    full_weights = lax.all_gather(weights, "feat", axis=0, tiled=True)
+    full_weights = jnp.concatenate(
+        lax.all_to_all(jnp.stack([weights] * lax.axis_size("feat")), "feat", 0, 0), axis=0
+    )
     scale = 2.0 * all_student.shape[0] * DS
     grad_student = scale * lax.dot_general(
         full_weights, all_student, (((0,), (0,)), ((), ())), preferred_element_type=jnp.float32

time: 575 us -> 558 us (0.970)
  waiting for transfers between devices: 439 us -> 415 us
    all_gather x1 -> x0, waiting for transfers between devices: 71.7 us -> none  [local(): full_weights = lax.all_gather(weights, 'feat', axis=0, tiled=True)]
    all_to_all x0 -> x1, waiting for transfers between devices: none -> 47.9 us  [local(): lax.all_to_all(jnp.stack([weights] * lax.axis_size('feat')), 'feat', 0, 0)]
where the time goes in v1:
time: 558 us
  waiting for transfers between devices  415 us (74%)
  blocking collectives  78.7 us (14%)
  matrix products  28.5 us (5%)
  between operations  17 us (3%)
  other arithmetic  11.1 us (2%)
    reduce_scatter x1, waiting for transfers between devices, local(): lax.psum_scatter(jnp.concatenate([gram_tile(all_teacher, teacher), gram_t...  195 us
    all_gather x1, waiting for transfers between devices, local(): lax.all_gather(teacher, 'tok', axis=0, tiled=True)  90.2 us
    all_gather x1, waiting for transfers between devices, local(): lax.all_gather(student, 'tok', axis=0, tiled=True)  80.1 us
    psum x1, blocking collectives, local(): lax.psum((local_sums[0], local_sums[1], local_sums[2]), ('tok', 'feat'))  78.7 us
    all_to_all x1, waiting for transfers between devices, local(): lax.all_to_all(jnp.stack([weights] * lax.axis_size('feat')), 'feat', 0, 0)  47.9 us
    dot_general x2, matrix products, gram_tile(): lax.dot_general(rows, mine, (((1,), (1,)), ((), ())), preferred_element_t...  19 us
  transfers between devices with their start and end apart: 4, of which 4 were waited for; matrix products, arithmetic and copies ran while one was open for 2% of the time, Pallas kernels for 0%

profile of v1, /device:TPU:1, one launch (start us, length us, event | category | flops | bytes accessed | tf_op | source)
XLA Modules:
  0.0 557.5 jit_solution(4334936151077504822)
XLA Ops:
  7.2 0.0 all-gather.5.cloned.1.call-start
  7.2 0.7 all-gather.5.cloned.1.call-update
  7.9 0.0 all-gather.3.cloned.1.call-start
  7.9 0.7 all-gather.3.cloned.1.call-update
  8.6 0.0 copy-start.1
  8.7 0.0 reduce-scatter.2.cloned.1.call-start
  8.7 80.1 %all-gather.5.cloned.1.call-done = bf16[8192,640]{1,0:T(8,128)(2,1)} async-done(((bf16[256,640]{1,0:T(8,128)(2,1)}), bf16[8192,640]{1,0:T(8,128)(2,1)}) %all-gather.5.cloned.1.call-update) | async-done | bytes 10485776 | tf_op jit(solution)/shard_map/all_gather | solution.py:17
  88.8 10.7 %fusion.1 = f32[8192,256]{0,1:T(8,128)} fusion(bf16[8192,640]{1,0:T(8,128)(2,1)} %all-gather.5.cloned.1.call-done, bf16[256,640]{1,0:T(8,128)(2,1)} %param.3), kind=kOutput, calls=%fused_computation.7 | convolution fusion | flops 2684354560 | bytes 19202048 | tf_op jit(solution)/shard_map/dot_general | solution.py:10
  99.5 90.2 %all-gather.3.cloned.1.call-done = bf16[8192,1024]{1,0:T(8,128)(2,1)} async-done(((bf16[256,1024]{1,0:T(8,128)(2,1)}), bf16[8192,1024]{1,0:T(8,128)(2,1)}) %all-gather.3.cloned.1.call-update) | async-done | bytes 16777232 | tf_op jit(solution)/shard_map/all_gather | solution.py:16
  189.8 0.0 copy-done.1
  189.8 0.0 copy-start
  189.8 8.3 %fusion = f32[8192,256]{0,1:T(8,128)S(1)} fusion(bf16[8192,1024]{1,0:T(8,128)(2,1)} %all-gather.3.cloned.1.call-done, bf16[256,1024]{1,0:T(8,128)(2,1)S(1)} %copy-done.1), kind=kOutput, calls=%fused_computation.6 | convolution fusion | flops 4294967296 | bytes 25690112 | tf_op jit(solution)/shard_map/dot_general | solution.py:10
  198.1 0.0 copy-done
  198.1 6.3 %pad_maximum_fusion = f32[8192,512]{0,1:T(8,128)} fusion(f32[8192,256]{0,1:T(8,128)S(1)} %copy-done, f32[8192,256]{0,1:T(8,128)S(1)} %fusion), kind=kLoop, calls=%fused_computation | loop fusion | flops 4194304 | bytes 33554432 | tf_op jit(solution)/shard_map/concatenate | solution.py:20
  204.4 0.0 reduce-scatter.2.cloned.1.call-update
  204.4 195.4 %reduce-scatter.2.cloned.1.call-done = f32[1024,512]{0,1:T(8,128)} async-done(((f32[8192,512]{0,1:T(8,128)}), f32[1024,512]{0,1:T(8,128)}) %reduce-scatter.2.cloned.1.call-update) | async-done | bytes 2097168 | tf_op jit(solution)/shard_map/reduce_scatter | solution.py:19
  399.8 2.4 multiply_reduce_fusion
  402.2 78.7 %all-reduce = (f32[]{:T(128)}, f32[]{:T(128)}, f32[]{:T(128)}) all-reduce(f32[]{:T(128)} %get-tuple-element.3, f32[]{:T(128)} %get-tuple-element.4, f32[]{:T(128)} %get-tuple-element.2), channel_id=1, replica_groups=mesh['tok'=32,'feat'=8] {'tok','feat'}, use_global_device_ids=true, to_apply=%region_2.0 | all-reduce | flops 3 | bytes 24 | tf_op jit(solution)/shard_map/psum | solution.py:28
  482.3 2.4 add_convert_fusion
  484.7 0.2 copy.4
  484.9 2.2 stack.2
  487.2 4.5 all-to-all-start
  492.4 47.9 %all-to-all-done = bf16[8,1024,256]{2,1,0:T(8,128)(2,1)} async-done(((bf16[8,1024,256]{2,1,0:T(8,128)(2,1)}), bf16[8,1024,256]{2,1,0:T(8,128)(2,1)}, u32[]{:S(2)}, u32[]{:S(2)}) %all-to-all-start) | async-done | bytes 4194336 | tf_op jit(solution)/shard_map/all_to_all | solution.py:34
  540.3 9.6 %convolution_multiply_fusion = f32[256,640]{1,0:T(8,128)} fusion(bf16[8192,256]{1,0:T(8,128)(2,1)} %bitcast, bf16[8192,640]{1,0:T(8,128)(2,1)} %all-gather.5.cloned.1.call-done), kind=kOutput, calls=%fused_computation.1 | convolution fusion | flops 2684518400 | bytes 15335424 | tf_op jit(solution)/shard_map/dot_general | solution.py:37
Async XLA Ops:
  7.2 81.7 %all-gather.5.cloned.1.call-start = ((), (), s32[]{:S(2)}) async-start(), calls=%async_computation.3 | async-start | bytes 10813440 | tf_op jit(solution)/shard_map/all_gather | solution.py:17
  7.9 181.9 %all-gather.3.cloned.1.call-start = ((), (), s32[]{:S(2)}) async-start(), calls=%async_computation.2 | async-start | bytes 17301504 | tf_op jit(solution)/shard_map/all_gather | solution.py:16
  8.6 181.1 %copy-start.1 = (bf16[256,1024]{1,0:T(8,128)(2,1)S(1)}, bf16[256,1024]{1,0:T(8,128)(2,1)}, u32[]{:S(2)}) copy-start(bf16[256,1024]{1,0:T(8,128)(2,1)} %param.2) | copy-start | bytes 1572868
  8.7 391.1 %reduce-scatter.2.cloned.1.call-start = ((), (), s32[]{:S(2)}) async-start(), calls=%async_computation.4 | async-start | bytes 18874368 | tf_op jit(solution)/shard_map/reduce_scatter | solution.py:19
  189.8 8.3 %copy-start = (f32[8192,256]{0,1:T(8,128)S(1)}, f32[8192,256]{0,1:T(8,128)}, u32[]{:S(2)}) copy-start(f32[8192,256]{0,1:T(8,128)} %fusion.1) | copy-start | bytes 25165828
  487.2 53.2 %all-to-all-start = ((bf16[8,1024,256]{2,1,0:T(8,128)(2,1)}), bf16[8,1024,256]{2,1,0:T(8,128)(2,1)}, u32[]{:S(2)}, u32[]{:S(2)}) async-start(bf16[8,1024,256]{2,1,0:T(8,128)(2,1)} %stack.2), calls=%async_computation.1 | async-start | bytes 8388608 | tf_op jit(solution)/shard_map/all_to_all | solution.py:34
Sparse Core Ops, SparseCore 0:
  9.9 78.9 all-gather.4
  90.7 99.0 all-gather.2
  204.5 195.1 reduce-scatter.1

commit v2 on v0

--- a/solution.py
+++ b/solution.py
@@ -25,7 +25,9 @@
     kern = parts[:, :width]
     lern = parts[:, width:]
     local_sums = (jnp.sum(kern * lern), jnp.sum(kern * kern), jnp.sum(lern * lern))
-    cross, ksq, lsq = lax.psum((local_sums[0], local_sums[1], local_sums[2]), ("tok", "feat"))
+    cross, ksq, lsq = lax.psum(
+        lax.psum((local_sums[0], local_sums[1], local_sums[2]), "tok"), "feat"
+    )
     knorm = jnp.sqrt(ksq)
     lnorm = jnp.sqrt(lsq)
     loss = -cross / (knorm * lnorm)

time: 575 us -> 571 us (level)
    psum x1 -> x2, blocking collectives: 78.7 us -> 76.2 us  [the longest x1 57 us: local(): lax.psum((local_sums[0], local_sums[1], local_sums[2]), 'tok')]
where the time goes in v2:
time: 571 us
  waiting for transfers between devices  438 us (77%)
  blocking collectives  76.2 us (13%)
  matrix products  28.5 us (5%)
  between operations  16.9 us (3%)
  other arithmetic  11.8 us (2%)
    reduce_scatter x1, waiting for transfers between devices, local(): lax.psum_scatter(jnp.concatenate([gram_tile(all_teacher, teacher), gram_t...  194 us
    all_gather x1, waiting for transfers between devices, local(): lax.all_gather(teacher, 'tok', axis=0, tiled=True)  90.2 us
    all_gather x1, waiting for transfers between devices, local(): lax.all_gather(student, 'tok', axis=0, tiled=True)  80.1 us
    all_gather x1, waiting for transfers between devices, local(): full_weights = lax.all_gather(weights, 'feat', axis=0, tiled=True)  71.8 us
    psum x1, blocking collectives, local(): lax.psum((local_sums[0], local_sums[1], local_sums[2]), 'tok')  57 us
    psum x1, blocking collectives, local(): lax.psum(lax.psum((local_sums[0], local_sums[1], local_sums[2]), 'tok'),...  19.2 us
    dot_general x2, matrix products, gram_tile(): lax.dot_general(rows, mine, (((1,), (1,)), ((), ())), preferred_element_t...  19 us
  transfers between devices with their start and end apart: 4, of which 4 were waited for; matrix products, arithmetic and copies ran while one was open for 2% of the time, Pallas kernels for 0%

profile of v2, /device:TPU:1, one launch (start us, length us, event | category | flops | bytes accessed | tf_op | source)
XLA Modules:
  0.0 571.0 jit_solution(2836844664184944750)
XLA Ops:
  7.2 0.0 all-gather.6.cloned.1.call-start
  7.2 0.7 all-gather.6.cloned.1.call-update
  7.9 0.0 all-gather.4.cloned.1.call-start
  7.9 0.7 all-gather.4.cloned.1.call-update
  8.6 0.0 copy-start.1
  8.7 0.0 reduce-scatter.2.cloned.1.call-start
  8.7 80.1 %all-gather.6.cloned.1.call-done = bf16[8192,640]{1,0:T(8,128)(2,1)} async-done(((bf16[256,640]{1,0:T(8,128)(2,1)}), bf16[8192,640]{1,0:T(8,128)(2,1)}) %all-gather.6.cloned.1.call-update) | async-done | bytes 10485776 | tf_op jit(solution)/shard_map/all_gather | solution.py:17
  88.8 10.7 %fusion.1 = f32[8192,256]{0,1:T(8,128)} fusion(bf16[8192,640]{1,0:T(8,128)(2,1)} %all-gather.6.cloned.1.call-done, bf16[256,640]{1,0:T(8,128)(2,1)} %param.3), kind=kOutput, calls=%fused_computation.7 | convolution fusion | flops 2684354560 | bytes 19202048 | tf_op jit(solution)/shard_map/dot_general | solution.py:10
  99.5 90.2 %all-gather.4.cloned.1.call-done = bf16[8192,1024]{1,0:T(8,128)(2,1)} async-done(((bf16[256,1024]{1,0:T(8,128)(2,1)}), bf16[8192,1024]{1,0:T(8,128)(2,1)}) %all-gather.4.cloned.1.call-update) | async-done | bytes 16777232 | tf_op jit(solution)/shard_map/all_gather | solution.py:16
  189.8 0.0 copy-done.1
  189.8 0.0 copy-start
  189.8 8.3 %fusion = f32[8192,256]{0,1:T(8,128)S(1)} fusion(bf16[8192,1024]{1,0:T(8,128)(2,1)} %all-gather.4.cloned.1.call-done, bf16[256,1024]{1,0:T(8,128)(2,1)S(1)} %copy-done.1), kind=kOutput, calls=%fused_computation.6 | convolution fusion | flops 4294967296 | bytes 25690112 | tf_op jit(solution)/shard_map/dot_general | solution.py:10
  198.1 0.0 copy-done
  198.1 6.2 %pad_maximum_fusion = f32[8192,512]{0,1:T(8,128)} fusion(f32[8192,256]{0,1:T(8,128)S(1)} %copy-done, f32[8192,256]{0,1:T(8,128)S(1)} %fusion), kind=kLoop, calls=%fused_computation | loop fusion | flops 4194304 | bytes 33554432 | tf_op jit(solution)/shard_map/concatenate | solution.py:20
  204.3 0.0 reduce-scatter.2.cloned.1.call-update
  204.3 0.0 all-gather.8.cloned.1.call-start
  204.4 193.9 %reduce-scatter.2.cloned.1.call-done = f32[1024,512]{0,1:T(8,128)} async-done(((f32[8192,512]{0,1:T(8,128)}), f32[1024,512]{0,1:T(8,128)}) %reduce-scatter.2.cloned.1.call-update) | async-done | bytes 2097168 | tf_op jit(solution)/shard_map/reduce_scatter | solution.py:19
  398.3 2.4 multiply_reduce_fusion
  400.7 57.0 %all-reduce = (f32[]{:T(128)}, f32[]{:T(128)}, f32[]{:T(128)}) all-reduce(f32[]{:T(128)} %get-tuple-element.3, f32[]{:T(128)} %get-tuple-element.4, f32[]{:T(128)} %get-tuple-element.2), channel_id=1, replica_groups=mesh['tok'=32,'feat'=8] {'tok'}, use_global_device_ids=true, to_apply=%region_2.0 | all-reduce | flops 3 | bytes 24 | tf_op jit(solution)/shard_map/psum | solution.py:29
  457.7 19.2 %all-reduce.1 = (f32[]{:T(128)}, f32[]{:T(128)}, f32[]{:T(128)}) all-reduce(f32[]{:T(128)} %get-tuple-element.5, f32[]{:T(128)} %get-tuple-element.6, f32[]{:T(128)} %get-tuple-element.7), channel_id=1, replica_groups=mesh['tok'=32,'feat'=8] {'feat'}, use_global_device_ids=true, to_apply=%region_3.0 | all-reduce | flops 3 | bytes 24 | tf_op jit(solution)/shard_map/psum | solution.py:28
  478.2 3.2 add_convert_fusion
  481.4 0.0 all-gather.8.cloned.1.call-update
  482.1 71.8 %all-gather.8.cloned.1.call-done = bf16[8192,256]{0,1:T(8,128)(2,1)} async-done(((bf16[1024,256]{0,1:T(8,128)(2,1)}), bf16[8192,256]{0,1:T(8,128)(2,1)}) %all-gather.8.cloned.1.call-update) | async-done | bytes 4194320 | tf_op jit(solution)/shard_map/all_gather | solution.py:35
  553.9 9.5 %convolution_multiply_fusion = f32[256,640]{1,0:T(8,128)} fusion(bf16[8192,256]{0,1:T(8,128)(2,1)} %all-gather.8.cloned.1.call-done, bf16[8192,640]{1,0:T(8,128)(2,1)} %all-gather.6.cloned.1.call-done), kind=kOutput, calls=%fused_computation.1 | convolution fusion | flops 2684518400 | bytes 15335424 | tf_op jit(solution)/shard_map/dot_general | solution.py:37
Async XLA Ops:
  7.2 81.7 %all-gather.6.cloned.1.call-start = ((), (), s32[]{:S(2)}) async-start(), calls=%async_computation.2 | async-start | bytes 10813440 | tf_op jit(solution)/shard_map/all_gather | solution.py:17
  7.9 181.9 %all-gather.4.cloned.1.call-start = ((), (), s32[]{:S(2)}) async-start(), calls=%async_computation.1 | async-start | bytes 17301504 | tf_op jit(solution)/shard_map/all_gather | solution.py:16
  8.6 181.1 %copy-start.1 = (bf16[256,1024]{1,0:T(8,128)(2,1)S(1)}, bf16[256,1024]{1,0:T(8,128)(2,1)}, u32[]{:S(2)}) copy-start(bf16[256,1024]{1,0:T(8,128)(2,1)} %param.2) | copy-start | bytes 1572868
  8.7 389.6 %reduce-scatter.2.cloned.1.call-start = ((), (), s32[]{:S(2)}) async-start(), calls=%async_computation.3 | async-start | bytes 18874368 | tf_op jit(solution)/shard_map/reduce_scatter | solution.py:19
  189.8 8.3 %copy-start = (f32[8192,256]{0,1:T(8,128)S(1)}, f32[8192,256]{0,1:T(8,128)}, u32[]{:S(2)}) copy-start(f32[8192,256]{0,1:T(8,128)} %fusion.1) | copy-start | bytes 25165828
  204.3 349.5 %all-gather.8.cloned.1.call-start = ((), (), s32[]{:S(2)}) async-start(), calls=%async_computation.4 | async-start | bytes 4718592 | tf_op jit(solution)/shard_map/all_gather | solution.py:35
Sparse Core Ops, SparseCore 0:
  9.9 78.9 all-gather.5
  90.7 99.0 all-gather.3
  204.4 193.8 reduce-scatter.1
  481.5 72.2 all-gather.7
